TPU v7x, 512 devices: a whole 4x8x8 slice. The times are simulated.
512 devices in a mesh: section: 128 (over z_hi, y, x, core), tensor: 4 (over z_lo).
Axes of the slice: x: 4, y: 8, z: 8 (z_hi: 2, z_lo: 4; z = z_hi * 4 + z_lo), core: 2. Of those that a mesh axis runs over, the one named last changes fastest.
Arguments:
- inputs: bfloat16 [32768, 6144], P('section', 'tensor'), may hold values from -6 to 6
- cotangent: bfloat16 [32768, 6144], P('section', 'tensor'), may hold values from -6 to 6
- ffn_weights: bfloat16 [3, 14336, 6144], P(None, 'section', 'tensor'), may hold values from -0.078125 to 0.078125
Outputs:
- input_grads: bfloat16 [32768, 6144], P('section', 'tensor')
- weight_grads: bfloat16 [3, 14336, 6144], P(None, 'section', 'tensor')
All inputs are finite; a program needn't handle non-finite values.
Results may differ from a plain program's by a relative error of at most 0.0049.
Values may be sent and summed in bfloat16 or wider, within the bound.
A program may use at most 64 MiB of HBM per device.

v0:
```python
import jax
import jax.numpy as jnp
from jax import lax
from jax.sharding import PartitionSpec as P

HOPS = 4


def shifted(x, axis, by):
    size = lax.axis_size(axis)
    return lax.ppermute(x, axis, [(i, (i + by) % size) for i in range(size)])


def local_pass(inputs, cotangent, blocks):
    projected = jnp.einsum("rd,khd->krh", inputs, blocks[:2], preferred_element_type=jnp.float32)
    grad_part = jnp.einsum("rd,hd->rh", cotangent, blocks[2], preferred_element_type=jnp.float32)
    gate_value, up_value, hidden_grad = lax.psum((projected[0], projected[1], grad_part), "tensor")
    sigmoid_gate = jax.nn.sigmoid(gate_value)
    silu_gate = gate_value * sigmoid_gate
    hidden = (silu_gate * up_value).astype(jnp.bfloat16)
    up_grad = (hidden_grad * silu_gate).astype(jnp.bfloat16)
    gate_grad = (
        hidden_grad * up_value * sigmoid_gate * (1.0 + gate_value * (1.0 - sigmoid_gate))
    ).astype(jnp.bfloat16)
    pair_grads = jnp.stack([gate_grad, up_grad])
    weight_terms = jnp.einsum("krh,rd->khd", pair_grads, inputs, preferred_element_type=jnp.float32)
    down_term = jnp.einsum("rh,rd->hd", hidden, cotangent, preferred_element_type=jnp.float32)
    input_term = jnp.einsum(
        "krh,khd->rd", pair_grads, blocks[:2], preferred_element_type=jnp.float32
    )
    return (jnp.concatenate([weight_terms, down_term[None]], 0), input_term)


def local(inputs, cotangent, ffn_weights):
    blocks = ffn_weights
    grad_terms = []
    input_total = jnp.zeros((inputs.shape[0], inputs.shape[1]), jnp.float32)
    for hop_index in range(HOPS):
        if hop_index > 0:
            blocks = shifted(blocks, "section", 1)
        terms, input_term = local_pass(inputs, cotangent, blocks)
        grad_terms.append(terms)
        input_total = input_total + input_term
    input_grads = input_total.astype(jnp.bfloat16)
    running = grad_terms[HOPS - 1]
    for hop_index in range(HOPS - 2, -1, -1):
        running = shifted(running, "section", -1) + grad_terms[hop_index]
    return (input_grads, running.astype(jnp.bfloat16))


def solution(mesh):
    in_specs = (P("section", "tensor"), P("section", "tensor"), P(None, "section", "tensor"))
    out_specs = (P("section", "tensor"), P(None, "section", "tensor"))
    return jax.shard_map(local, mesh=mesh, in_specs=in_specs, out_specs=out_specs, check_vma=False)
```

profile of v0, /device:TPU:63, one launch (start us, length us, event | category | flops | bytes accessed | tf_op | source)
XLA Modules:
  0.0 382.1 jit_solution(10070241731288266912)
XLA Ops:
  7.2 10.4 %collective-permute-start = (bf16[3,112,1536]{2,1,0:T(8,128)(2,1)}, bf16[3,112,1536]{2,1,0:T(8,128)(2,1)S(1)}, u32[]{:S(2)}, u32[]{:S(2)}) collective-permute-start(bf16[3,112,1536]{2,1,0:T(8,128)(2,1)} %param.5), channel_id=1, source_target_pairs={{0,4},{4,8},{8,12},{12,16},{16,20},{20,24},{24,28},{28,32},{32,36}... | collective-permute-start | bytes 3096584 | tf_op jit(solution)/shard_map/ppermute | solution.py:11
  17.7 21.0 %collective-permute-done = bf16[3,112,1536]{2,1,0:T(8,128)(2,1)S(1)} collective-permute-done((bf16[3,112,1536]{2,1,0:T(8,128)(2,1)}, bf16[3,112,1536]{2,1,0:T(8,128)(2,1)S(1)}, u32[]{:S(2)}, u32[]{:S(2)}) %collective-permute-start) | collective-permute-done | bytes 1032224 | tf_op jit(solution)/shard_map/ppermute | solution.py:11
  38.7 14.4 %collective-permute-start.1 = (bf16[3,112,1536]{2,1,0:T(8,128)(2,1)S(1)}, bf16[3,112,1536]{2,1,0:T(8,128)(2,1)S(1)}, u32[]{:S(2)}, u32[]{:S(2)}) collective-permute-start(bf16[3,112,1536]{2,1,0:T(8,128)(2,1)S(1)} %collective-permute-done), channel_id=1, source_target_pairs={{0,4},{4,8},{8,12},{12,16},{16,20},{20,24},{24,28},{28,32},{32,36}... | collective-permute-start | bytes 3096584 | tf_op jit(solution)/shard_map/ppermute | solution.py:11
  53.2 1.5 convolution_bitcast_fusion.11
  55.4 1.0 fusion.24
  56.8 16.7 %collective-permute-done.1 = bf16[3,112,1536]{2,1,0:T(8,128)(2,1)S(1)} collective-permute-done((bf16[3,112,1536]{2,1,0:T(8,128)(2,1)S(1)}, bf16[3,112,1536]{2,1,0:T(8,128)(2,1)S(1)}, u32[]{:S(2)}, u32[]{:S(2)}) %collective-permute-start.1) | collective-permute-done | bytes 1032224 | tf_op jit(solution)/shard_map/ppermute | solution.py:11
  73.5 14.8 %collective-permute-start.2 = (bf16[3,112,1536]{2,1,0:T(8,128)(2,1)S(1)}, bf16[3,112,1536]{2,1,0:T(8,128)(2,1)S(1)}, u32[]{:S(2)}, u32[]{:S(2)}) collective-permute-start(bf16[3,112,1536]{2,1,0:T(8,128)(2,1)S(1)} %collective-permute-done.1), channel_id=1, source_target_pairs={{0,4},{4,8},{8,12},{12,16},{16,20},{20,24},{24,28},{28,32},{32,36}... | collective-permute-start | bytes 3096584 | tf_op jit(solution)/shard_map/ppermute | solution.py:11
  89.1 1.0 fusion.23
  91.2 1.0 fusion.22
  92.2 18.7 %collective-permute-done.2 = bf16[3,112,1536]{2,1,0:T(8,128)(2,1)S(1)} collective-permute-done((bf16[3,112,1536]{2,1,0:T(8,128)(2,1)S(1)}, bf16[3,112,1536]{2,1,0:T(8,128)(2,1)S(1)}, u32[]{:S(2)}, u32[]{:S(2)}) %collective-permute-start.2) | collective-permute-done | bytes 1032224 | tf_op jit(solution)/shard_map/ppermute | solution.py:11
  111.3 0.7 slice_bitcast_fusion.7
  112.1 1.0 fusion.21
  113.1 86.8 %all-reduce.3.cloned.1.call-done = (f32[256,112]{0,1:T(8,128)}, f32[256,112]{0,1:T(8,128)}, f32[256,112]{0,1:T(8,128)}, f32[256,112]{0,1:T(8,128)}, f32[256,112]...) async-done(((f32[256,112]{0,1:T(8,128)}, ...) | async-done | bytes 1376272 | tf_op jit(solution)/shard_map/psum | solution.py:17
  199.9 1.3 convolution_bitcast_fusion.7
  201.8 3.0 collective-permute-start.3
  205.6 54.3 %collective-permute-done.3 = f32[3,112,1536]{2,1,0:T(8,128)S(1)} collective-permute-done((f32[3,112,1536]{2,1,0:T(8,128)S(1)}, f32[3,112,1536]{2,1,0:T(8,128)S(1)}, u32[]{:S(2)}, u32[]{:S(2)}) %collective-permute-start.3) | collective-permute-done | bytes 2064416 | tf_op jit(solution)/shard_map/ppermute | solution.py:11
  260.2 2.1 collective-permute-start.4
  263.0 54.7 %collective-permute-done.4 = f32[3,112,1536]{2,1,0:T(8,128)S(1)} collective-permute-done((f32[3,112,1536]{2,1,0:T(8,128)S(1)}, f32[3,112,1536]{2,1,0:T(8,128)S(1)}, u32[]{:S(2)}, u32[]{:S(2)}) %collective-permute-start.4) | collective-permute-done | bytes 2064416 | tf_op jit(solution)/shard_map/ppermute | solution.py:11
  318.0 1.9 collective-permute-start.5
  322.1 0.8 copy-done.8
  323.3 0.8 copy-done.4
  324.1 1.3 fusion.3
  325.4 48.6 %collective-permute-done.5 = f32[3,112,1536]{2,1,0:T(8,128)S(1)} collective-permute-done((f32[3,112,1536]{2,1,0:T(8,128)S(1)}, f32[3,112,1536]{2,1,0:T(8,128)S(1)}, u32[]{:S(2)}, u32[]{:S(2)}) %collective-permute-start.5) | collective-permute-done | bytes 2064416 | tf_op jit(solution)/shard_map/ppermute | solution.py:11
  374.0 1.2 fusion.4
  (65 shorter events, 8.5 us)
Async XLA Ops:
  7.2 46.0 %copy-start = (bf16[256,1536]{1,0:T(8,128)(2,1)S(1)}, bf16[256,1536]{1,0:T(8,128)(2,1)}, u32[]{:S(2)}) copy-start(bf16[256,1536]{1,0:T(8,128)(2,1)} %param.3) | copy-start | bytes 2359300
  7.2 48.2 %copy-start.2 = (bf16[3,112,1536]{2,1,0:T(8,128)(2,1)S(1)}, bf16[3,112,1536]{2,1,0:T(8,128)(2,1)}, u32[]{:S(2)}) copy-start(bf16[3,112,1536]{2,1,0:T(8,128)(2,1)} %param.5) | copy-start | bytes 3096580
  7.2 48.2 %copy-start.1 = (bf16[256,1536]{1,0:T(8,128)(2,1)S(1)}, bf16[256,1536]{1,0:T(8,128)(2,1)}, u32[]{:S(2)}) copy-start(bf16[256,1536]{1,0:T(8,128)(2,1)} %param.4) | copy-start | bytes 2359300
  7.2 192.7 %all-reduce.3.cloned.1.call-start = ((), (), s32[]{:S(2)}) async-start(), calls=%async_computation | async-start | bytes 2752512 | tf_op jit(solution)/shard_map/psum | solution.py:17
  7.2 31.5 %collective-permute-start = (bf16[3,112,1536]{2,1,0:T(8,128)(2,1)}, bf16[3,112,1536]{2,1,0:T(8,128)(2,1)S(1)}, u32[]{:S(2)}, u32[]{:S(2)}) collective-permute-start(bf16[3,112,1536]{2,1,0:T(8,128)(2,1)} %param.5), channel_id=1, source_target_pairs={{0,4},{4,8},{8,12},{12,16},{16,20},{20,24},{24,28},{28,32},{32,36}... | collective-permute-start | bytes 3096584 | tf_op jit(solution)/shard_map/ppermute | solution.py:11
  38.7 50.3 %copy-start.5 = (bf16[3,112,1536]{2,1,0:T(8,128)(2,1)}, bf16[3,112,1536]{2,1,0:T(8,128)(2,1)S(1)}, u32[]{:S(2)}) copy-start(bf16[3,112,1536]{2,1,0:T(8,128)(2,1)S(1)} %collective-permute-done) | copy-start | bytes 3096580
  38.7 34.7 %collective-permute-start.1 = (bf16[3,112,1536]{2,1,0:T(8,128)(2,1)S(1)}, bf16[3,112,1536]{2,1,0:T(8,128)(2,1)S(1)}, u32[]{:S(2)}, u32[]{:S(2)}) collective-permute-start(bf16[3,112,1536]{2,1,0:T(8,128)(2,1)S(1)} %collective-permute-done), channel_id=1, source_target_pairs={{0,4},{4,8},{8,12},{12,16},{16,20},{20,24},{24,28},{28,32},{32,36}... | collective-permute-start | bytes 3096584 | tf_op jit(solution)/shard_map/ppermute | solution.py:11
  73.5 17.7 %copy-start.7 = (bf16[3,112,1536]{2,1,0:T(8,128)(2,1)}, bf16[3,112,1536]{2,1,0:T(8,128)(2,1)S(1)}, u32[]{:S(2)}) copy-start(bf16[3,112,1536]{2,1,0:T(8,128)(2,1)S(1)} %collective-permute-done.1) | copy-start | bytes 3096580
  73.5 37.4 %collective-permute-start.2 = (bf16[3,112,1536]{2,1,0:T(8,128)(2,1)S(1)}, bf16[3,112,1536]{2,1,0:T(8,128)(2,1)S(1)}, u32[]{:S(2)}, u32[]{:S(2)}) collective-permute-start(bf16[3,112,1536]{2,1,0:T(8,128)(2,1)S(1)} %collective-permute-done.1), channel_id=1, source_target_pairs={{0,4},{4,8},{8,12},{12,16},{16,20},{20,24},{24,28},{28,32},{32,36}... | collective-permute-start | bytes 3096584 | tf_op jit(solution)/shard_map/ppermute | solution.py:11
  110.9 2.2 copy-start.3
  199.9 1.3 copy-start.16
  199.9 1.3 copy-start.20
  201.7 3.2 copy-start.13
  201.7 3.2 copy-start.14
  201.8 3.3 copy-start.19
  201.8 58.0 %collective-permute-start.3 = (f32[3,112,1536]{2,1,0:T(8,128)S(1)}, f32[3,112,1536]{2,1,0:T(8,128)S(1)}, u32[]{:S(2)}, u32[]{:S(2)}) collective-permute-start(f32[3,112,1536]{2,1,0:T(8,128)S(1)} %pad_maximum_fusion), channel_id=1, source_target_pairs={{0,508},{4,0},{8,4},{12,8},{16,12},{20,16},{24,20},{28,24},{32,28}... | collective-permute-start | bytes 6193160 | tf_op jit(solution)/shard_map/ppermute | solution.py:11
  205.5 56.7 %copy-start.11 = (f32[256,112]{0,1:T(8,128)S(1)}, f32[256,112]{0,1:T(8,128)}, u32[]{:S(2)}) copy-start(f32[256,112]{0,1:T(8,128)} %get-tuple-element.6) | copy-start | bytes 344068
  205.6 56.7 %copy-start.12 = (f32[256,112]{0,1:T(8,128)S(1)}, f32[256,112]{0,1:T(8,128)}, u32[]{:S(2)}) copy-start(f32[256,112]{0,1:T(8,128)} %get-tuple-element.7) | copy-start | bytes 344068
  260.2 2.4 copy-start.18
  260.2 57.5 %collective-permute-start.4 = (f32[3,112,1536]{2,1,0:T(8,128)S(1)}, f32[3,112,1536]{2,1,0:T(8,128)S(1)}, u32[]{:S(2)}, u32[]{:S(2)}) collective-permute-start(f32[3,112,1536]{2,1,0:T(8,128)S(1)} %maximum_add_fusion), channel_id=1, source_target_pairs={{0,508},{4,0},{8,4},{12,8},{16,12},{20,16},{24,20},{28,24},{32,28}... | collective-permute-start | bytes 6193160 | tf_op jit(solution)/shard_map/ppermute | solution.py:11
  263.0 57.0 %copy-start.9 = (f32[256,112]{0,1:T(8,128)S(1)}, f32[256,112]{0,1:T(8,128)}, u32[]{:S(2)}) copy-start(f32[256,112]{0,1:T(8,128)} %get-tuple-element.3) | copy-start | bytes 344068
  263.0 57.0 %copy-start.10 = (f32[256,112]{0,1:T(8,128)S(1)}, f32[256,112]{0,1:T(8,128)}, u32[]{:S(2)}) copy-start(f32[256,112]{0,1:T(8,128)} %get-tuple-element.4) | copy-start | bytes 344068
  263.0 57.0 %copy-start.17 = (f32[256,112]{0,1:T(8,128)S(1)}, f32[256,112]{0,1:T(8,128)}, u32[]{:S(2)}) copy-start(f32[256,112]{0,1:T(8,128)} %get-tuple-element.2) | copy-start | bytes 344068
  318.0 56.0 %collective-permute-start.5 = (f32[3,112,1536]{2,1,0:T(8,128)S(1)}, f32[3,112,1536]{2,1,0:T(8,128)S(1)}, u32[]{:S(2)}, u32[]{:S(2)}) collective-permute-start(f32[3,112,1536]{2,1,0:T(8,128)S(1)} %maximum_add_fusion.1), channel_id=1, source_target_pairs={{0,508},{4,0},{8,4},{12,8},{16,12},{20,16},{24,20},{28,24},{32,28}... | collective-permute-start | bytes 6193160 | tf_op jit(solution)/shard_map/ppermute | solution.py:11
  (4 other events, 4.9 us)
Sparse Core Ops, SparseCore 0:
  113.2 86.6 all-reduce.2
where the time goes:
time: 383 us; the launch traced here: 382 us
  waiting for transfers between devices  301 us (79%)
  starting transfers between devices  46.7 us (12%)
  between operations  14.4 us (4%)
  matrix products  12.7 us (3%)
  local copies, waits for them, and re-layouts  5.21 us (1%)
    ppermute x6, waiting for transfers between devices, shifted(): return lax.ppermute(x, axis, [(i, (i + by) % size) for i in range(size)])  214 us
    psum x1, waiting for transfers between devices, local_pass(): lax.psum((projected[0], projected[1], grad_part), 'tensor')  86.8 us
    ppermute x6, starting transfers between devices, shifted(): return lax.ppermute(x, axis, [(i, (i + by) % size) for i in range(size)])  46.6 us
  transfers between devices with their start and end apart: 7, of which 7 were waited for; matrix products, arithmetic and copies ran while one was open for 3% of the time, Pallas kernels for 0%

commit v1 on v0

v1 whole, which is shorter than its diff:
```python
import functools

import jax
import jax.numpy as jnp
from jax import lax
from jax.experimental import pallas as pl
from jax.experimental.pallas import tpu as pltpu
from jax.sharding import PartitionSpec as P

MESH = pl.DeviceIdType.MESH
F32 = jnp.float32
BF16 = jnp.bfloat16

W_MATE, W_NEXT, W_NEXT_BACK, W_LAST, W_LAST_BACK, X_BACK, Y_BACK, PART_A, PART_B, DW_BACK, DX_NEXT = range(11)


def dot_nt(a, b):
    return lax.dot_general(a, b, (((1,), (1,)), ((), ())), preferred_element_type=F32)


def dot_nn(a, b):
    return jnp.dot(a, b, preferred_element_type=F32)


def kernel(
    n_section, n_tensor, tile,
    x_ref, y_ref, wt_ref, gx_ref, gw_ref,
    w, xf, yf, part, rs_out, rs_in, ag, agt, dw0, dxa, pa, pb, ca, dxf, sp, sc, sx,
    msg_s, msg_r, rs_s, rs_r, ag_s, ag_r,
):
    section, me_t = lax.axis_index("section"), lax.axis_index("tensor")
    even = lax.rem(section, 2) == 0
    odd = jnp.logical_not(even)
    tokens, depth = x_ref.shape
    height, padded = wt_ref.shape[1], w.shape[2]
    rows = tokens // n_tensor

    def at(by):
        return (lax.rem(section + by + n_section, n_section), me_t)

    def peer(by):
        return (section, lax.rem(me_t + by, n_tensor))

    def rows_of(t):
        return pl.ds(pl.multiple_of(t * rows, rows), rows)

    def message(kind, src, dst, to):
        return pltpu.make_async_remote_copy(
            src_ref=src, dst_ref=dst, send_sem=msg_s.at[kind], recv_sem=msg_r.at[kind],
            device_id=to, device_id_type=MESH,
        )

    def slot(i):
        return w.at[i, :, pl.ds(0, height), :]

    w_mate = message(W_MATE, wt_ref, slot(3), at(1))
    w_next = message(W_NEXT, wt_ref, slot(1), at(3))
    w_next_back = message(W_NEXT_BACK, slot(1), slot(1), at(-1))
    w_last = message(W_LAST, wt_ref, slot(2), at(1))
    w_last_back = message(W_LAST_BACK, slot(2), slot(2), at(1))
    x_back = message(X_BACK, x_ref, xf, at(-2))
    y_back = message(Y_BACK, y_ref, yf, at(-2))
    part_a_even = message(PART_A, sp.at[0], pa, at(1))
    part_a_odd = message(PART_A, sp.at[0], pa, at(-1))
    part_b = message(PART_B, sp.at[1], pb, at(-1))
    dw_back_even = message(DW_BACK, sc, ca, at(-1))
    dw_back_odd = message(DW_BACK, sc, ca, at(-3))
    dx_next = message(DX_NEXT, sx, dxf, at(2))

    barrier = pltpu.get_barrier_semaphore()

    def greet(to):
        pl.semaphore_signal(barrier, inc=1, device_id=to, device_id_type=MESH)

    for by in range(1, n_tensor):
        greet(peer(by))

    @pl.when(even)
    def _():
        for by in (1, -1, 3, -2, 2):
            greet(at(by))

    @pl.when(odd)
    def _():
        for by in (-1, 1, -3):
            greet(at(by))

    for i in range(4):
        w[i, :, height:, :] = jnp.zeros((3, padded - height, depth), BF16)
    w[0, :, :height, :] = wt_ref[...]

    @pl.when(even)
    def _():
        pl.semaphore_wait(barrier, n_tensor - 1 + 5)

    @pl.when(odd)
    def _():
        pl.semaphore_wait(barrier, n_tensor - 1 + 3)

    def rs_copy(st, by):
        return pltpu.make_async_remote_copy(
            src_ref=rs_out.at[st, rows_of(lax.rem(me_t + by, n_tensor))], dst_ref=rs_in.at[st, by - 1],
            send_sem=rs_s.at[st, by - 1], recv_sem=rs_r.at[st, by - 1],
            device_id=peer(by), device_id_type=MESH,
        )

    def ag_copy(st, by):
        return pltpu.make_async_remote_copy(
            src_ref=ag.at[st, rows_of(me_t)], dst_ref=ag.at[st, rows_of(me_t)],
            send_sem=ag_s.at[st, by - 1], recv_sem=ag_r.at[st, by - 1],
            device_id=peer(by), device_id_type=MESH,
        )

    def ag_arrival(st, by):
        src_t = lax.rem(me_t - by + n_tensor, n_tensor)
        return pltpu.make_async_remote_copy(
            src_ref=ag.at[st, rows_of(src_t)], dst_ref=ag.at[st, rows_of(src_t)],
            send_sem=ag_s.at[st, by - 1], recv_sem=ag_r.at[st, by - 1],
            device_id=peer(by), device_id_type=MESH,
        )

    def forward(st, x, y, i):
        gu = dot_nt(x[...], w[i, 0:2].reshape(2 * padded, depth))
        part[st, :, : 2 * padded] = gu
        rs_out[st, :, : 2 * padded] = gu.astype(BF16)
        d = dot_nt(y[...], w[i, 2])
        part[st, :, 2 * padded :] = d
        rs_out[st, :, 2 * padded :] = d.astype(BF16)
        for by in range(1, n_tensor):
            rs_copy(st, by).start()

    def middle(st):
        for by in range(1, n_tensor):
            rs_copy(st, by).wait_recv()
        own = rows_of(me_t)
        total = part[st, own, :]
        for by in range(1, n_tensor):
            total = total + rs_in[st, by - 1].astype(F32)
        g, u, dh = total[:, :padded], total[:, padded : 2 * padded], total[:, 2 * padded :]
        sig = jax.nn.sigmoid(g)
        silu = g * sig
        ag[st, own, :padded] = (dh * u * sig * (1.0 + g * (1.0 - sig))).astype(BF16)
        ag[st, own, padded : 2 * padded] = (dh * silu).astype(BF16)
        ag[st, own, 2 * padded :] = (silu * u).astype(BF16)
        for by in range(1, n_tensor):
            ag_copy(st, by).start()

    def gathered(st):
        for by in range(1, n_tensor):
            ag_arrival(st, by).wait_recv()
        agt[st] = ag[st].T

    def weight_terms(pairs, emit):
        @pl.loop(0, depth // tile)
        def _(j):
            cols = pl.ds(pl.multiple_of(j * tile, tile), tile)
            gu = sum(dot_nn(agt[st, : 2 * padded], x[:, cols]) for st, x, _ in pairs)
            emit(0, cols, gu[:height])
            emit(1, cols, gu[padded : padded + height])
            emit(2, cols, sum(dot_nn(agt[st, 2 * padded :], y[:, cols]) for st, _, y in pairs)[:height])

    def input_terms(pairs, emit):
        @pl.loop(0, depth // tile)
        def _(j):
            cols = pl.ds(pl.multiple_of(j * tile, tile), tile)
            emit(
                cols,
                sum(
                    dot_nn(ag[st, :, : 2 * padded], w[i, 0:2, :, cols].reshape(2 * padded, tile))
                    for st, i in pairs
                ),
            )

    def to_f32(ref):
        def emit(k, cols, value):
            ref[k, :, cols] = value

        return emit

    def to_bf16(ref):
        def emit(k, cols, value):
            ref[k, :, cols] = value.astype(BF16)

        return emit

    def dx_acc(cols, value):
        dxa[:, cols] = value

    @pl.when(even)
    def _():
        w_next.start()
        x_back.start()
        y_back.start()
        w_mate.start()
        forward(0, x_ref, y_ref, 0)
        middle(0)
        gathered(0)
        weight_terms([(0, x_ref, y_ref)], to_f32(dw0))
        w_next_back.wait_recv()
        forward(1, x_ref, y_ref, 1)
        middle(1)
        gathered(1)
        weight_terms([(1, x_ref, y_ref)], to_bf16(sp.at[0]))
        part_a_even.start()
        input_terms([(0, 0), (1, 1)], dx_acc)
        x_back.wait_recv()
        y_back.wait_recv()
        w_last.wait_recv()
        w_last_back.start()
        forward(3, xf, yf, 2)
        forward(2, x_ref, y_ref, 2)
        middle(3)
        middle(2)
        gathered(3)

        def dx_out(cols, value):
            sx[:, cols] = value.astype(BF16)

        input_terms([(3, 2)], dx_out)
        dx_next.start()
        gathered(2)

        def dw_f32(k, cols, value):
            part_dw = value
            sc[k, :, cols] = (part_dw + pb[k, :, cols].astype(F32)).astype(BF16)

        part_b.wait_recv()
        weight_terms([(2, x_ref, y_ref), (3, xf, yf)], dw_f32)
        dw_back_even.start()
        dx_next.wait_recv()

        def dx_last(cols, value):
            gx_ref[:, cols] = (dxa[:, cols] + dxf[:, cols].astype(F32) + value).astype(BF16)

        input_terms([(2, 2)], dx_last)
        part_a_odd.wait_recv()
        dw_back_odd.wait_recv()
        for k in range(3):
            gw_ref[k] = (dw0[k] + pa[k].astype(F32) + ca[k].astype(F32)).astype(BF16)
        for copy in (w_next, x_back, y_back, w_mate, part_a_even, w_last_back, dx_next, dw_back_even):
            copy.wait_send()

    @pl.when(odd)
    def _():
        forward(0, x_ref, y_ref, 0)
        w_mate.wait_recv()
        forward(1, x_ref, y_ref, 3)
        middle(0)
        middle(1)
        gathered(0)
        gathered(1)
        weight_terms([(1, x_ref, y_ref)], to_bf16(sp.at[0]))
        part_a_odd.start()
        w_next.wait_recv()
        w_last.start()
        w_next_back.start()
        forward(2, x_ref, y_ref, 1)
        weight_terms([(0, x_ref, y_ref)], to_f32(dw0))
        middle(2)
        gathered(2)
        part_a_even.wait_recv()

        def dw_sum(k, cols, value):
            sc[k, :, cols] = (value + pa[k, :, cols].astype(F32)).astype(BF16)

        weight_terms([(2, x_ref, y_ref)], dw_sum)
        dw_back_odd.start()
        input_terms([(0, 0), (1, 3), (2, 1)], dx_acc)
        w_last_back.wait_recv()
        forward(3, x_ref, y_ref, 2)
        middle(3)
        gathered(3)
        weight_terms([(3, x_ref, y_ref)], to_bf16(sp.at[1]))
        part_b.start()

        def dx_last(cols, value):
            gx_ref[:, cols] = (dxa[:, cols] + value).astype(BF16)

        input_terms([(3, 2)], dx_last)
        dw_back_even.wait_recv()
        for k in range(3):
            gw_ref[k] = (dw0[k] + ca[k].astype(F32)).astype(BF16)
        for copy in (part_a_odd, w_last, w_next_back, dw_back_odd, part_b):
            copy.wait_send()

    for st in range(4):
        for by in range(1, n_tensor):
            rs_copy(st, by).wait_send()
            ag_copy(st, by).wait_send()


def solution(mesh):
    n_section, n_tensor = mesh.shape["section"], mesh.shape["tensor"]

    def local(x, y, weights):
        tokens, depth = x.shape
        height = weights.shape[1]
        padded = -(-height // 128) * 128
        rows = tokens // n_tensor
        tile = min(depth, 512)
        vmem = pl.BlockSpec(memory_space=pltpu.VMEM)
        return pl.pallas_call(
            functools.partial(kernel, n_section, n_tensor, tile),
            out_shape=(
                jax.ShapeDtypeStruct((tokens, depth), BF16),
                jax.ShapeDtypeStruct((3, height, depth), BF16),
            ),
            in_specs=[vmem] * 3,
            out_specs=(vmem, vmem),
            scratch_shapes=[
                pltpu.VMEM((4, 3, padded, depth), BF16),
                pltpu.VMEM((tokens, depth), BF16),
                pltpu.VMEM((tokens, depth), BF16),
                pltpu.VMEM((4, tokens, 3 * padded), F32),
                pltpu.VMEM((4, tokens, 3 * padded), BF16),
                pltpu.VMEM((4, n_tensor - 1, rows, 3 * padded), BF16),
                pltpu.VMEM((4, tokens, 3 * padded), BF16),
                pltpu.VMEM((4, 3 * padded, tokens), BF16),
                pltpu.VMEM((3, height, depth), F32),
                pltpu.VMEM((tokens, depth), F32),
                pltpu.VMEM((3, height, depth), BF16),
                pltpu.VMEM((3, height, depth), BF16),
                pltpu.VMEM((3, height, depth), BF16),
                pltpu.VMEM((tokens, depth), BF16),
                pltpu.VMEM((2, 3, height, depth), BF16),
                pltpu.VMEM((3, height, depth), BF16),
                pltpu.VMEM((tokens, depth), BF16),
                pltpu.SemaphoreType.DMA((11,)),
                pltpu.SemaphoreType.DMA((11,)),
                pltpu.SemaphoreType.DMA((4, n_tensor - 1)),
                pltpu.SemaphoreType.DMA((4, n_tensor - 1)),
                pltpu.SemaphoreType.DMA((4, n_tensor - 1)),
                pltpu.SemaphoreType.DMA((4, n_tensor - 1)),
            ],
            compiler_params=pltpu.CompilerParams(
                collective_id=0, has_side_effects=True, vmem_limit_bytes=52 * 2**20
            ),
            cost_estimate=pl.CostEstimate(
                flops=2 * 8 * 4 * tokens * height * depth,
                bytes_accessed=2 * 2 * (3 * tokens * depth + 6 * height * depth),
                transcendentals=4 * tokens * height,
            ),
        )(x, y, weights)

    return jax.shard_map(
        local,
        mesh=mesh,
        in_specs=(P("section", "tensor"), P("section", "tensor"), P(None, "section", "tensor")),
        out_specs=(P("section", "tensor"), P(None, "section", "tensor")),
        check_vma=False,
    )
```

time: 383 us -> 162 us (0.42)
  the two profiles are of different devices: /device:TPU:63 before, /device:TPU:55 now
where the time goes in v1:
time: 162 us
  Pallas kernels  158 us (98%)
  local copies, waits for them, and re-layouts  3.58 us (2%)
    pallas_call x1, Pallas kernels, local(): pl.pallas_call(functools.partial(kernel, n_section, n_tensor, tile), out_...  158 us
    unnamed x6, local copies, waits for them, and re-layouts  3.58 us

profile of v1, /device:TPU:55, one launch (start us, length us, event | category | flops | bytes accessed | tf_op | source)
XLA Modules:
  0.0 162.0 jit_solution(3398749122845458217)
XLA Ops:
  0.6 0.0 copy-start
  0.6 1.1 copy-done
  1.8 157.8 %shard_map.50 = (bf16[256,1536]{1,0:T(8,128)(2,1)S(1)}, bf16[3,112,1536]{2,1,0:T(8,128)(2,1)}) custom-call(bf16[256,1536]{1,0:T(8,128)(2,1)S(1)} %copy-done, bf16[256,1536]{1,0:T(8,128)(2,1)} %y_ref.1, bf16[3,112,1536]{2,1,0:T(8,128)(2,1)} %wt_ref.1), custom_call_target="tpu_custom_call" | custom-call | flops 2818572288 | bytes 8847360 | tf_op jit(solution)/shard_map/pallas_call | solution.py:302
  159.6 0.0 copy-start.1
  159.6 0.9 copy.7
  160.4 0.6 copy-done.1
  161.1 1.0 copy.8
Async XLA Ops:
  0.6 1.1 copy-start
  159.6 1.5 copy-start.1

commit v2 on v1

--- a/solution.py
+++ b/solution.py
@@ -13,6 +13,40 @@
 
 W_MATE, W_NEXT, W_NEXT_BACK, W_LAST, W_LAST_BACK, X_BACK, Y_BACK, PART_A, PART_B, DW_BACK, DX_NEXT = range(11)
 
+HALF = 64
+LAST_EVEN, LAST_ODD, FIRST_EVEN, FIRST_ODD = 62, 63, 0, 1
+ROUTES = {
+    "next_1": (LAST_EVEN, 49, FIRST_ODD, 1, 1, 1),
+    "next_2": (LAST_EVEN, 41, FIRST_ODD, 1, 2, 1),
+    "last_1": (LAST_ODD, 33, FIRST_EVEN, 1, 1, 1),
+    "last_2": (LAST_ODD, 25, FIRST_EVEN, 1, 2, 1),
+    "dx_1": (LAST_EVEN, 49, FIRST_EVEN, 1, 6, 5),
+    "dx_2": (LAST_EVEN, 41, FIRST_EVEN, 1, 11, 5),
+    "x_1": (FIRST_EVEN, 15, LAST_EVEN, -1, 4, 6),
+    "x_2": (FIRST_EVEN, 23, LAST_EVEN, -1, 10, 6),
+    "y_1": (FIRST_EVEN, 31, LAST_EVEN, -1, 4, 6),
+    "y_2": (FIRST_EVEN, 39, LAST_EVEN, -1, 10, 6),
+    "dw_even_1": (FIRST_EVEN, 15, LAST_ODD, -1, 1, 1),
+    "dw_even_2": (FIRST_EVEN, 39, LAST_ODD, -1, 2, 1),
+    "dw_odd_1": (FIRST_ODD, 23, LAST_EVEN, -1, 1, 1),
+    "dw_odd_2": (FIRST_ODD, 31, LAST_EVEN, -1, 2, 1),
+}
+
+
+def route_steps(name):
+    sender, relay, receiver, halves = ROUTES[name][:4]
+    return relay - sender + HALF * halves, receiver - relay
+
+
+def route_greetings():
+    found = {}
+    for name, (sender, relay, receiver, *_) in ROUTES.items():
+        there, on = route_steps(name)
+        for place, by in ((sender, there), (relay, -there), (relay, on), (receiver, -on)):
+            if by not in found.setdefault(place, []):
+                found[place].append(by)
+    return found
+
 
 def dot_nt(a, b):
     return lax.dot_general(a, b, (((1,), (1,)), ((), ())), preferred_element_type=F32)
@@ -26,7 +60,8 @@
     n_section, n_tensor, tile,
     x_ref, y_ref, wt_ref, gx_ref, gw_ref,
     w, xf, yf, part, rs_out, rs_in, ag, agt, dw0, dxa, pa, pb, ca, dxf, sp, sc, sx,
-    msg_s, msg_r, rs_s, rs_r, ag_s, ag_r,
+    hold_w, hold_dx, hold_xy, hold_dw,
+    msg_s, msg_r, hold_s, hold_r, rs_s, rs_r, ag_s, ag_r, go,
 ):
     section, me_t = lax.axis_index("section"), lax.axis_index("tensor")
     even = lax.rem(section, 2) == 0
@@ -34,6 +69,8 @@
     tokens, depth = x_ref.shape
     height, padded = wt_ref.shape[1], w.shape[2]
     rows = tokens // n_tensor
+    place = lax.rem(section, HALF)
+    early = section < HALF
 
     def at(by):
         return (lax.rem(section + by + n_section, n_section), me_t)
@@ -52,6 +89,64 @@
 
     def slot(i):
         return w.at[i, :, pl.ds(0, height), :]
+
+    def relayed(kind, name, src, hold, dst):
+        there_by, on_by = route_steps(name)
+        sem = list(ROUTES).index(name)
+        unit = 1 if len(src.shape) == 3 else 16
+        first, size = (n * unit for n in ROUTES[name][4:])
+        part, hold = pl.ds(first, size), hold.at[pl.ds(0, size)]
+        there = pltpu.make_async_remote_copy(
+            src_ref=src.at[part], dst_ref=hold, send_sem=msg_s.at[kind], recv_sem=hold_r.at[sem],
+            device_id=at(there_by), device_id_type=MESH,
+        )
+        on = pltpu.make_async_remote_copy(
+            src_ref=hold, dst_ref=dst.at[part], send_sem=hold_s.at[sem], recv_sem=msg_r.at[kind],
+            device_id=at(on_by), device_id_type=MESH,
+        )
+        return ROUTES[name][1], there, on
+
+    def split(kind, name, src, hold, dst, to):
+        names = [n for n in ROUTES if n.rsplit("_", 1)[0] == name]
+        whole = src.shape[0]
+        unit = 1 if len(src.shape) == 3 else 16
+        size = whole - unit * sum(ROUTES[n][5] for n in names)
+        part = pl.ds(0, size)
+        first = message(kind, src.at[part], dst.at[part], to) if size else None
+        return first, [relayed(kind, n, src, hold, dst) for n in names]
+
+    def start_parts(*messages):
+        for first, _ in messages:
+            if first is not None:
+                first.start()
+        parts = [one for _, more in messages for one in more]
+
+        @pl.when(me_t < n_tensor // 2)
+        def _():
+            for one in parts:
+                one[1].start()
+
+        @pl.when(me_t >= n_tensor // 2)
+        def _():
+            for one in parts[::-1]:
+                one[1].start()
+
+    def send(copy, at_place, parts):
+        @pl.when(place != at_place)
+        def _():
+            copy.start()
+
+        @pl.when(place == at_place)
+        def _():
+            start_parts(parts)
+
+    def relay(copies, when=True):
+        where, there, on = copies
+
+        @pl.when((place == where) & when)
+        def _():
+            there.wait_recv()
+            on.start()
 
     w_mate = message(W_MATE, wt_ref, slot(3), at(1))
     w_next = message(W_NEXT, wt_ref, slot(1), at(3))
@@ -67,6 +162,22 @@
     dw_back_odd = message(DW_BACK, sc, ca, at(-3))
     dx_next = message(DX_NEXT, sx, dxf, at(2))
 
+    next_parts = split(W_NEXT, "next", wt_ref, hold_w.at[0], slot(1), at(3))
+    last_parts = split(W_LAST, "last", wt_ref, hold_w.at[1], slot(2), at(1))
+    dx_parts = split(DX_NEXT, "dx", sx, hold_dx, dxf, at(2))
+    x_parts = split(X_BACK, "x", x_ref, hold_xy.at[0], xf, at(-2))
+    y_parts = split(Y_BACK, "y", y_ref, hold_xy.at[1], yf, at(-2))
+    dwe_parts = split(DW_BACK, "dw_even", sc, hold_dw.at[0], ca, at(-1))
+    dwo_parts = split(DW_BACK, "dw_odd", sc, hold_dw.at[1], ca, at(-3))
+    all_parts = (next_parts, last_parts, dx_parts, x_parts, y_parts, dwe_parts, dwo_parts)
+
+    def relay_all(messages, when=True):
+        for _, more in messages:
+            for one in more:
+                relay(one, when)
+
+    late = jnp.logical_not(early)
+
     barrier = pltpu.get_barrier_semaphore()
 
     def greet(to):
@@ -85,17 +196,21 @@
         for by in (-1, 1, -3):
             greet(at(by))
 
+    for where, others in route_greetings().items():
+
+        @pl.when(place == where)
+        def _(others=others):
+            for by in others:
+                greet(at(by))
+
     for i in range(4):
         w[i, :, height:, :] = jnp.zeros((3, padded - height, depth), BF16)
     w[0, :, :height, :] = wt_ref[...]
 
-    @pl.when(even)
-    def _():
-        pl.semaphore_wait(barrier, n_tensor - 1 + 5)
-
-    @pl.when(odd)
-    def _():
-        pl.semaphore_wait(barrier, n_tensor - 1 + 3)
+    expected = jnp.where(even, n_tensor - 1 + 5, n_tensor - 1 + 3)
+    for where, others in route_greetings().items():
+        expected = expected + jnp.where(place == where, len(others), 0)
+    pl.semaphore_wait(barrier, expected)
 
     def rs_copy(st, by):
         return pltpu.make_async_remote_copy(
@@ -151,18 +266,16 @@
         agt[st] = ag[st].T
 
     def weight_terms(pairs, emit):
-        @pl.loop(0, depth // tile)
-        def _(j):
-            cols = pl.ds(pl.multiple_of(j * tile, tile), tile)
+        for j in range(0, depth, tile):
+            cols = pl.ds(j, tile)
             gu = sum(dot_nn(agt[st, : 2 * padded], x[:, cols]) for st, x, _ in pairs)
             emit(0, cols, gu[:height])
             emit(1, cols, gu[padded : padded + height])
             emit(2, cols, sum(dot_nn(agt[st, 2 * padded :], y[:, cols]) for st, _, y in pairs)[:height])
 
     def input_terms(pairs, emit):
-        @pl.loop(0, depth // tile)
-        def _(j):
-            cols = pl.ds(pl.multiple_of(j * tile, tile), tile)
+        for j in range(0, depth, tile):
+            cols = pl.ds(j, tile)
             emit(
                 cols,
                 sum(
@@ -188,14 +301,24 @@
 
     @pl.when(even)
     def _():
-        w_next.start()
-        x_back.start()
-        y_back.start()
         w_mate.start()
+        send(w_next, LAST_EVEN, next_parts)
+
+        @pl.when(place != FIRST_EVEN)
+        def _():
+            x_back.start()
+            y_back.start()
+
+        @pl.when(place == FIRST_EVEN)
+        def _():
+            start_parts(x_parts, y_parts)
+
         forward(0, x_ref, y_ref, 0)
         middle(0)
         gathered(0)
         weight_terms([(0, x_ref, y_ref)], to_f32(dw0))
+        w_next.wait_send()
+        pl.semaphore_signal(go, inc=1, device_id=at(1), device_id_type=MESH)
         w_next_back.wait_recv()
         forward(1, x_ref, y_ref, 1)
         middle(1)
@@ -203,10 +326,10 @@
         weight_terms([(1, x_ref, y_ref)], to_bf16(sp.at[0]))
         part_a_even.start()
         input_terms([(0, 0), (1, 1)], dx_acc)
+        w_last.wait_recv()
+        w_last_back.start()
         x_back.wait_recv()
         y_back.wait_recv()
-        w_last.wait_recv()
-        w_last_back.start()
         forward(3, xf, yf, 2)
         forward(2, x_ref, y_ref, 2)
         middle(3)
@@ -217,16 +340,15 @@
             sx[:, cols] = value.astype(BF16)
 
         input_terms([(3, 2)], dx_out)
-        dx_next.start()
+        send(dx_next, LAST_EVEN, dx_parts)
         gathered(2)
-
-        def dw_f32(k, cols, value):
-            part_dw = value
-            sc[k, :, cols] = (part_dw + pb[k, :, cols].astype(F32)).astype(BF16)
-
         part_b.wait_recv()
-        weight_terms([(2, x_ref, y_ref), (3, xf, yf)], dw_f32)
-        dw_back_even.start()
+
+        def dw_sum(k, cols, value):
+            sc[k, :, cols] = (value + pb[k, :, cols].astype(F32)).astype(BF16)
+
+        weight_terms([(2, x_ref, y_ref), (3, xf, yf)], dw_sum)
+        send(dw_back_even, FIRST_EVEN, dwe_parts)
         dx_next.wait_recv()
 
         def dx_last(cols, value):
@@ -237,11 +359,15 @@
         dw_back_odd.wait_recv()
         for k in range(3):
             gw_ref[k] = (dw0[k] + pa[k].astype(F32) + ca[k].astype(F32)).astype(BF16)
-        for copy in (w_next, x_back, y_back, w_mate, part_a_even, w_last_back, dx_next, dw_back_even):
+        for copy in (x_back, y_back, w_mate, part_a_even, w_last_back, dx_next, dw_back_even):
             copy.wait_send()
 
     @pl.when(odd)
     def _():
+        @pl.when(place == LAST_ODD)
+        def _():
+            start_parts(last_parts)
+
         forward(0, x_ref, y_ref, 0)
         w_mate.wait_recv()
         forward(1, x_ref, y_ref, 3)
@@ -251,8 +377,15 @@
         gathered(1)
         weight_terms([(1, x_ref, y_ref)], to_bf16(sp.at[0]))
         part_a_odd.start()
+        relay_all((x_parts, y_parts, next_parts, last_parts), late)
+        pl.semaphore_wait(go, 1)
+
+        @pl.when(place != LAST_ODD)
+        def _():
+            w_last.start()
+
         w_next.wait_recv()
-        w_last.start()
+
         w_next_back.start()
         forward(2, x_ref, y_ref, 1)
         weight_terms([(0, x_ref, y_ref)], to_f32(dw0))
@@ -264,24 +397,36 @@
             sc[k, :, cols] = (value + pa[k, :, cols].astype(F32)).astype(BF16)
 
         weight_terms([(2, x_ref, y_ref)], dw_sum)
-        dw_back_odd.start()
+        send(dw_back_odd, FIRST_ODD, dwo_parts)
         input_terms([(0, 0), (1, 3), (2, 1)], dx_acc)
+        relay_all((x_parts, y_parts, next_parts), early)
         w_last_back.wait_recv()
         forward(3, x_ref, y_ref, 2)
         middle(3)
         gathered(3)
         weight_terms([(3, x_ref, y_ref)], to_bf16(sp.at[1]))
         part_b.start()
+        relay_all((last_parts,), early)
+        relay_all((dx_parts, dwo_parts), late)
 
         def dx_last(cols, value):
             gx_ref[:, cols] = (dxa[:, cols] + value).astype(BF16)
 
         input_terms([(3, 2)], dx_last)
+        relay_all((dx_parts, dwo_parts), early)
+        relay_all((dwe_parts,))
         dw_back_even.wait_recv()
         for k in range(3):
             gw_ref[k] = (dw0[k] + ca[k].astype(F32)).astype(BF16)
         for copy in (part_a_odd, w_last, w_next_back, dw_back_odd, part_b):
             copy.wait_send()
+
+    for _, more in all_parts:
+        for copies in more:
+
+            @pl.when(place == copies[0])
+            def _(copies=copies):
+                copies[2].wait_send()
 
     for st in range(4):
         for by in range(1, n_tensor):
@@ -325,12 +470,19 @@
                 pltpu.VMEM((2, 3, height, depth), BF16),
                 pltpu.VMEM((3, height, depth), BF16),
                 pltpu.VMEM((tokens, depth), BF16),
+                pltpu.VMEM((2, 1, height, depth), BF16),
+                pltpu.VMEM((tokens // 2, depth), BF16),
+                pltpu.VMEM((2, tokens // 2, depth), BF16),
+                pltpu.VMEM((2, 1, height, depth), BF16),
                 pltpu.SemaphoreType.DMA((11,)),
                 pltpu.SemaphoreType.DMA((11,)),
+                pltpu.SemaphoreType.DMA((len(ROUTES),)),
+                pltpu.SemaphoreType.DMA((len(ROUTES),)),
                 pltpu.SemaphoreType.DMA((4, n_tensor - 1)),
                 pltpu.SemaphoreType.DMA((4, n_tensor - 1)),
                 pltpu.SemaphoreType.DMA((4, n_tensor - 1)),
                 pltpu.SemaphoreType.DMA((4, n_tensor - 1)),
+                pltpu.SemaphoreType.REGULAR,
             ],
             compiler_params=pltpu.CompilerParams(
                 collective_id=0, has_side_effects=True, vmem_limit_bytes=52 * 2**20

time: 162 us -> 114 us (0.70)
  the two profiles are of different devices: /device:TPU:55 before, /device:TPU:383 now
where the time goes in v2:
time: 114 us
  Pallas kernels  110 us (96%)
  local copies, waits for them, and re-layouts  3.58 us (3%)
    pallas_call x1, Pallas kernels, local(): pl.pallas_call(functools.partial(kernel, n_section, n_tensor, tile), out_...  110 us
    unnamed x6, local copies, waits for them, and re-layouts  3.58 us

profile of v2, /device:TPU:383, one launch (start us, length us, event | category | flops | bytes accessed | tf_op | source)
XLA Modules:
  0.0 113.9 jit_solution(17786838407736629558)
XLA Ops:
  0.6 0.0 copy-start
  0.6 1.1 copy-done
  1.8 109.7 %shard_map.50 = (bf16[256,1536]{1,0:T(8,128)(2,1)S(1)}, bf16[3,112,1536]{2,1,0:T(8,128)(2,1)}) custom-call(bf16[256,1536]{1,0:T(8,128)(2,1)S(1)} %copy-done, bf16[256,1536]{1,0:T(8,128)(2,1)} %y_ref.1, bf16[3,112,1536]{2,1,0:T(8,128)(2,1)} %wt_ref.1), custom_call_target="tpu_custom_call" | custom-call | flops 2818572288 | bytes 8847360 | tf_op jit(solution)/shard_map/pallas_call | solution.py:447
  111.5 0.0 copy-start.1
  111.5 0.9 copy.7
  112.4 0.6 copy-done.1
  113.0 1.0 copy.8
Async XLA Ops:
  0.6 1.1 copy-start
  111.5 1.5 %copy-start.1 = (bf16[3,112,1536]{2,1,0:T(8,128)(2,1)S(1)}, bf16[3,112,1536]{2,1,0:T(8,128)(2,1)}, u32[]{:S(2)}) copy-start(bf16[3,112,1536]{2,1,0:T(8,128)(2,1)} %get-tuple-element.5) | copy-start | bytes 3096580

commit v3 on v2

--- a/solution.py
+++ b/solution.py
@@ -27,9 +27,9 @@
     "y_1": (FIRST_EVEN, 31, LAST_EVEN, -1, 4, 6),
     "y_2": (FIRST_EVEN, 39, LAST_EVEN, -1, 10, 6),
     "dw_even_1": (FIRST_EVEN, 15, LAST_ODD, -1, 1, 1),
-    "dw_even_2": (FIRST_EVEN, 39, LAST_ODD, -1, 2, 1),
-    "dw_odd_1": (FIRST_ODD, 23, LAST_EVEN, -1, 1, 1),
-    "dw_odd_2": (FIRST_ODD, 31, LAST_EVEN, -1, 2, 1),
+    "dw_even_2": (FIRST_EVEN, 23, LAST_ODD, -1, 2, 1),
+    "dw_odd_1": (FIRST_ODD, 31, LAST_EVEN, -1, 1, 1),
+    "dw_odd_2": (FIRST_ODD, 39, LAST_EVEN, -1, 2, 1),
 }
 
 
@@ -322,18 +322,18 @@
         w_next_back.wait_recv()
         forward(1, x_ref, y_ref, 1)
         middle(1)
-        gathered(1)
-        weight_terms([(1, x_ref, y_ref)], to_bf16(sp.at[0]))
-        part_a_even.start()
-        input_terms([(0, 0), (1, 1)], dx_acc)
         w_last.wait_recv()
         w_last_back.start()
         x_back.wait_recv()
         y_back.wait_recv()
         forward(3, xf, yf, 2)
         forward(2, x_ref, y_ref, 2)
+        gathered(1)
+        weight_terms([(1, x_ref, y_ref)], to_bf16(sp.at[0]))
+        part_a_even.start()
         middle(3)
         middle(2)
+        input_terms([(0, 0), (1, 1)], dx_acc)
         gathered(3)
 
         def dx_out(cols, value):
@@ -389,7 +389,11 @@
         w_next_back.start()
         forward(2, x_ref, y_ref, 1)
         weight_terms([(0, x_ref, y_ref)], to_f32(dw0))
+        relay_all((next_parts, last_parts), early)
         middle(2)
+        relay_all((x_parts, y_parts), early)
+        w_last_back.wait_recv()
+        forward(3, x_ref, y_ref, 2)
         gathered(2)
         part_a_even.wait_recv()
 
@@ -398,15 +402,11 @@
 
         weight_terms([(2, x_ref, y_ref)], dw_sum)
         send(dw_back_odd, FIRST_ODD, dwo_parts)
+        middle(3)
         input_terms([(0, 0), (1, 3), (2, 1)], dx_acc)
-        relay_all((x_parts, y_parts, next_parts), early)
-        w_last_back.wait_recv()
-        forward(3, x_ref, y_ref, 2)
-        middle(3)
         gathered(3)
         weight_terms([(3, x_ref, y_ref)], to_bf16(sp.at[1]))
         part_b.start()
-        relay_all((last_parts,), early)
         relay_all((dx_parts, dwo_parts), late)
 
         def dx_last(cols, value):

time: 114 us -> 99.9 us (0.88)
  the two profiles are of different devices: /device:TPU:383 before, /device:TPU:255 now
where the time goes in v3:
time: 99.9 us; the launch traced here: 99.6 us
  Pallas kernels  95.4 us (95%)
  local copies, waits for them, and re-layouts  3.58 us (4%)
    pallas_call x1, Pallas kernels, local(): pl.pallas_call(functools.partial(kernel, n_section, n_tensor, tile), out_...  95.4 us
    unnamed x6, local copies, waits for them, and re-layouts  3.58 us

profile of v3, /device:TPU:255, one launch (start us, length us, event | category | flops | bytes accessed | tf_op | source)
XLA Modules:
  0.0 99.6 jit_solution(4296832621945299300)
XLA Ops:
  0.6 0.0 copy-start
  0.6 1.1 %copy-done = bf16[256,1536]{1,0:T(8,128)(2,1)S(1)} copy-done((bf16[256,1536]{1,0:T(8,128)(2,1)S(1)}, bf16[256,1536]{1,0:T(8,128)(2,1)}, u32[]{:S(2)}) %copy-start) | copy-done | bytes 786456
  1.8 95.4 %shard_map.50 = (bf16[256,1536]{1,0:T(8,128)(2,1)S(1)}, bf16[3,112,1536]{2,1,0:T(8,128)(2,1)}) custom-call(bf16[256,1536]{1,0:T(8,128)(2,1)S(1)} %copy-done, bf16[256,1536]{1,0:T(8,128)(2,1)} %y_ref.1, bf16[3,112,1536]{2,1,0:T(8,128)(2,1)} %wt_ref.1), custom_call_target="tpu_custom_call" | custom-call | flops 2818572288 | bytes 8847360 | tf_op jit(solution)/shard_map/pallas_call | solution.py:447
  97.2 0.0 copy-start.1
  97.2 0.9 copy.7
  98.0 0.6 copy-done.1
  98.7 1.0 copy.8
Async XLA Ops:
  0.6 1.1 %copy-start = (bf16[256,1536]{1,0:T(8,128)(2,1)S(1)}, bf16[256,1536]{1,0:T(8,128)(2,1)}, u32[]{:S(2)}) copy-start(bf16[256,1536]{1,0:T(8,128)(2,1)} %x_ref.1) | copy-start | bytes 2359300
  97.2 1.5 %copy-start.1 = (bf16[3,112,1536]{2,1,0:T(8,128)(2,1)S(1)}, bf16[3,112,1536]{2,1,0:T(8,128)(2,1)}, u32[]{:S(2)}) copy-start(bf16[3,112,1536]{2,1,0:T(8,128)(2,1)} %get-tuple-element.5) | copy-start | bytes 3096580

commit v4 on v3

--- a/solution.py
+++ b/solution.py
@@ -26,10 +26,10 @@
     "x_2": (FIRST_EVEN, 23, LAST_EVEN, -1, 10, 6),
     "y_1": (FIRST_EVEN, 31, LAST_EVEN, -1, 4, 6),
     "y_2": (FIRST_EVEN, 39, LAST_EVEN, -1, 10, 6),
-    "dw_even_1": (FIRST_EVEN, 15, LAST_ODD, -1, 1, 1),
-    "dw_even_2": (FIRST_EVEN, 23, LAST_ODD, -1, 2, 1),
-    "dw_odd_1": (FIRST_ODD, 31, LAST_EVEN, -1, 1, 1),
-    "dw_odd_2": (FIRST_ODD, 39, LAST_EVEN, -1, 2, 1),
+    "dw_even_1": (FIRST_EVEN, 15, LAST_ODD, -1, 4, 2),
+    "dw_even_2": (FIRST_EVEN, 23, LAST_ODD, -1, 6, 1),
+    "dw_odd_1": (FIRST_ODD, 31, LAST_EVEN, -1, 2, 3),
+    "dw_odd_2": (FIRST_ODD, 39, LAST_EVEN, -1, 5, 2),
 }
 
 
@@ -90,12 +90,17 @@
     def slot(i):
         return w.at[i, :, pl.ds(0, height), :]
 
+    def rows_part(name, first, size):
+        if name.startswith("dw"):
+            return slice(None), pl.ds(16 * first, 16 * size)
+        unit = 1 if name.startswith(("next", "last")) else 16
+        return (pl.ds(unit * first, unit * size),)
+
     def relayed(kind, name, src, hold, dst):
         there_by, on_by = route_steps(name)
         sem = list(ROUTES).index(name)
-        unit = 1 if len(src.shape) == 3 else 16
-        first, size = (n * unit for n in ROUTES[name][4:])
-        part, hold = pl.ds(first, size), hold.at[pl.ds(0, size)]
+        part = rows_part(name, *ROUTES[name][4:])
+        hold = hold.at[rows_part(name, 0, ROUTES[name][5])]
         there = pltpu.make_async_remote_copy(
             src_ref=src.at[part], dst_ref=hold, send_sem=msg_s.at[kind], recv_sem=hold_r.at[sem],
             device_id=at(there_by), device_id_type=MESH,
@@ -108,11 +113,8 @@
 
     def split(kind, name, src, hold, dst, to):
         names = [n for n in ROUTES if n.rsplit("_", 1)[0] == name]
-        whole = src.shape[0]
-        unit = 1 if len(src.shape) == 3 else 16
-        size = whole - unit * sum(ROUTES[n][5] for n in names)
-        part = pl.ds(0, size)
-        first = message(kind, src.at[part], dst.at[part], to) if size else None
+        part = rows_part(name, 0, min(ROUTES[n][4] for n in names))
+        first = message(kind, src.at[part], dst.at[part], to)
         return first, [relayed(kind, n, src, hold, dst) for n in names]
 
     def start_parts(*messages):
@@ -473,7 +475,7 @@
                 pltpu.VMEM((2, 1, height, depth), BF16),
                 pltpu.VMEM((tokens // 2, depth), BF16),
                 pltpu.VMEM((2, tokens // 2, depth), BF16),
-                pltpu.VMEM((2, 1, height, depth), BF16),
+                pltpu.VMEM((2, 3, 48, depth), BF16),
                 pltpu.SemaphoreType.DMA((11,)),
                 pltpu.SemaphoreType.DMA((11,)),
                 pltpu.SemaphoreType.DMA((len(ROUTES),)),

time: 99.9 us -> 97.9 us (0.980)
  Pallas kernels: 95.4 us -> 93.4 us
    pallas_call x1, Pallas kernels: 95.4 us -> 93.4 us  [local(): pl.pallas_call(functools.partial(kernel, n_section, n_tensor, tile), out_...]
where the time goes in v4:
time: 97.9 us; the launch traced here: 97.6 us
  Pallas kernels  93.4 us (95%)
  local copies, waits for them, and re-layouts  3.58 us (4%)
    pallas_call x1, Pallas kernels, local(): pl.pallas_call(functools.partial(kernel, n_section, n_tensor, tile), out_...  93.4 us
    unnamed x6, local copies, waits for them, and re-layouts  3.58 us

profile of v4, /device:TPU:255, one launch (start us, length us, event | category | flops | bytes accessed | tf_op | source)
XLA Modules:
  0.0 97.6 jit_solution(12758016130343965621)
XLA Ops:
  0.6 0.0 copy-start
  0.6 1.1 %copy-done = bf16[256,1536]{1,0:T(8,128)(2,1)S(1)} copy-done((bf16[256,1536]{1,0:T(8,128)(2,1)S(1)}, bf16[256,1536]{1,0:T(8,128)(2,1)}, u32[]{:S(2)}) %copy-start) | copy-done | bytes 786456
  1.8 93.4 %shard_map.50 = (bf16[256,1536]{1,0:T(8,128)(2,1)S(1)}, bf16[3,112,1536]{2,1,0:T(8,128)(2,1)}) custom-call(bf16[256,1536]{1,0:T(8,128)(2,1)S(1)} %copy-done, bf16[256,1536]{1,0:T(8,128)(2,1)} %y_ref.1, bf16[3,112,1536]{2,1,0:T(8,128)(2,1)} %wt_ref.1), custom_call_target="tpu_custom_call" | custom-call | flops 2818572288 | bytes 8847360 | tf_op jit(solution)/shard_map/pallas_call | solution.py:449
  95.2 0.0 copy-start.1
  95.2 0.9 copy.7
  96.1 0.6 copy-done.1
  96.7 1.0 copy.8
Async XLA Ops:
  0.6 1.1 %copy-start = (bf16[256,1536]{1,0:T(8,128)(2,1)S(1)}, bf16[256,1536]{1,0:T(8,128)(2,1)}, u32[]{:S(2)}) copy-start(bf16[256,1536]{1,0:T(8,128)(2,1)} %x_ref.1) | copy-start | bytes 2359300
  95.2 1.5 %copy-start.1 = (bf16[3,112,1536]{2,1,0:T(8,128)(2,1)S(1)}, bf16[3,112,1536]{2,1,0:T(8,128)(2,1)}, u32[]{:S(2)}) copy-start(bf16[3,112,1536]{2,1,0:T(8,128)(2,1)} %get-tuple-element.5) | copy-start | bytes 3096580
